TPU v7x, 32 devices: a whole 2x2x4 slice. The times are simulated.
32 devices in a mesh: wide: 8 (over y, x, core), narrow: 4 (over z).
Axes of the slice: x: 2, y: 2, z: 4, core: 2. Of those that a mesh axis runs over, the one named last changes fastest.
Arguments:
- documents: bfloat16 [8192, 768], P('wide'), may hold values from -8 to 8
- label_weight: bfloat16 [4096, 768], P(('wide', 'narrow')), may hold values from -1 to 1
- sample_ids: int32 [4096], P(('wide', 'narrow')), may hold values from 0 to 2812280, as said below
- positive_cols: int32 [8192, 4], P('wide'), may hold values from 0 to 4095
- up_weight: bfloat16 [768, 3072], P(None, 'narrow'), may hold values from -0.21875 to 0.21875
- down_weight: bfloat16 [3072, 768], P('narrow'), may hold values from -0.109375 to 0.109375
Outputs:
- label_grad: float32 [4096, 768], P(('wide', 'narrow'))
- up_grad: float32 [768, 3072], P('wide', 'narrow')
- down_grad: float32 [3072, 768], P('narrow', 'wide')
Inputs may be any that keep to these rules, and one draw needn't show every extreme that they name: `sample_ids`: frequency ranks (0 is the most frequent of 2812281 labels), not falling along the sampled columns; frequent ranks repeat.
All inputs are finite; a program needn't handle non-finite values.
Results may differ from a plain program's by a relative error of at most 0.01.
Values may be sent and summed in bfloat16 or wider, within the bound.
A program may use at most 64 MiB of HBM per device.

v0:
```python
from functools import partial

import jax
import jax.numpy as jnp
from jax import lax
from jax.sharding import PartitionSpec as P

CATALOG = 2812281


def from_behind(block, axis, distance):
    devices = range(lax.axis_size(axis))
    route = [((i - distance) % len(devices), i) for i in devices]
    return lax.ppermute(block, axis, route)


def expected_log(rank_ids, sampled):
    rank_float = rank_ids.astype(jnp.float32)
    return (
        jnp.log(jnp.float32(sampled))
        + jnp.log(jnp.log1p(1.0 / (rank_float + 1.0)))
        - jnp.log(jnp.log(jnp.float32(CATALOG) + 1.0))
    )


def absorb(row_state, logits):
    run_max, run_sum = row_state
    new_max = jnp.maximum(run_max, jnp.max(logits, axis=1))
    run_sum = run_sum * jnp.exp(run_max - new_max) + jnp.sum(
        jnp.exp(logits - new_max[:, None]), axis=1
    )
    return (new_max, run_sum)


def local(documents, label_weight, sample_ids, positive_cols, up_weight, down_weight):
    wide_count = lax.axis_size("wide")
    narrow_count = lax.axis_size("narrow")
    wide_place = lax.axis_index("wide")
    narrow_place = lax.axis_index("narrow")
    lab_rows, model_width = label_weight.shape
    doc_rows = documents.shape[0]
    sampled = lab_rows * wide_count * narrow_count
    contract_rows = (((1,), (1,)), ((), ()))
    contract_first = (((0,), (0,)), ((), ()))
    pre_act = jnp.dot(documents, up_weight, preferred_element_type=jnp.float32)
    hidden = jax.nn.gelu(pre_act, approximate=False).astype(jnp.bfloat16)
    partial_out = jnp.dot(hidden, down_weight, preferred_element_type=jnp.float32)
    summed = lax.psum(partial_out, "narrow")
    embedding = (documents.astype(jnp.float32) + summed).astype(jnp.bfloat16)
    all_ranks = lax.all_gather(sample_ids, "wide", axis=0, tiled=True)
    log_expect = expected_log(all_ranks, sampled).reshape(wide_count, lab_rows)
    offsets = jnp.arange(lab_rows, dtype=jnp.int32)

    def block_logits(label_block, log_part):
        return (
            lax.dot_general(
                embedding, label_block, contract_rows, preferred_element_type=jnp.float32
            )
            - log_part[None, :]
        )

    start_state = (
        jnp.full((doc_rows,), -jnp.inf, jnp.float32),
        jnp.zeros((doc_rows,), jnp.float32),
    )
    stored_blocks = jnp.zeros((wide_count, lab_rows, model_width), jnp.bfloat16)
    half_rows = lab_rows // 2

    def visit_halves(up_source, down_source, upper_rows, lower_rows, carry):
        stored, row_state = carry
        stored = lax.dynamic_update_slice(stored, upper_rows[None], (up_source, 0, 0))
        stored = lax.dynamic_update_slice(stored, lower_rows[None], (down_source, half_rows, 0))
        label_block = jnp.concatenate([upper_rows, lower_rows], axis=0)
        log_part = jnp.concatenate(
            [log_expect[up_source][:half_rows], log_expect[down_source][half_rows:]]
        )
        return (stored, absorb(row_state, block_logits(label_block, log_part)))

    def travel_two(cycle_step, carry):
        upper_rows, lower_rows, stored, row_state = carry
        up_source = (wide_place - cycle_step) % wide_count
        down_source = (wide_place + cycle_step) % wide_count
        stored, row_state = visit_halves(
            up_source, down_source, upper_rows, lower_rows, (stored, row_state)
        )
        upper_rows = from_behind(upper_rows, "wide", 1)
        lower_rows = from_behind(lower_rows, "wide", -1)
        return (upper_rows, lower_rows, stored, row_state)

    upper_rows, lower_rows, stored_blocks, row_state = lax.fori_loop(
        0,
        wide_count - 1,
        travel_two,
        (label_weight[:half_rows], label_weight[half_rows:], stored_blocks, start_state),
    )
    stored_blocks, row_state = visit_halves(
        (wide_place + 1) % wide_count,
        (wide_place - 1) % wide_count,
        upper_rows,
        lower_rows,
        (stored_blocks, row_state),
    )
    run_max, run_sum = row_state
    row_top = lax.pmax(run_max, "narrow")
    row_total = lax.psum(run_sum * jnp.exp(run_max - row_top), "narrow")
    log_total = row_top + jnp.log(row_total)
    per_doc = positive_cols.shape[1]

    def gradient_block(source):
        label_block = stored_blocks[source]
        logits = block_logits(label_block, log_expect[source])
        columns = (source * narrow_count + narrow_place) * lab_rows + offsets
        positive_hits = jnp.sum(
            (positive_cols[:, :, None] == columns[None, None, :]).astype(jnp.float32), axis=1
        )
        grad_logits = (jnp.exp(logits - log_total[:, None]) - positive_hits / per_doc).astype(
            jnp.bfloat16
        )
        return (label_block, grad_logits)

    zero_docs = jnp.zeros((doc_rows, model_width), jnp.float32)

    def carry_home(cycle_step, carry):
        home_sum, embed_back = carry
        source = (wide_place - cycle_step - 1) % wide_count
        label_block, grad_logits = gradient_block(source)
        home_sum = home_sum + lax.dot_general(
            grad_logits, embedding, contract_first, preferred_element_type=jnp.float32
        )
        embed_back = embed_back + jnp.dot(
            grad_logits, label_block, preferred_element_type=jnp.float32
        )
        home_sum = from_behind(home_sum, "wide", 1)
        return (home_sum, embed_back)

    home_sum, embed_back = lax.fori_loop(
        0, wide_count - 1, carry_home, (jnp.zeros((lab_rows, model_width), jnp.float32), zero_docs)
    )
    label_block, grad_logits = gradient_block(wide_place)
    label_grad = home_sum + lax.dot_general(
        grad_logits, embedding, contract_first, preferred_element_type=jnp.float32
    )
    embed_back = embed_back + jnp.dot(grad_logits, label_block, preferred_element_type=jnp.float32)
    embed_grad = lax.psum(embed_back, "narrow").astype(jnp.bfloat16)
    act_grad = lax.dot_general(
        embed_grad, down_weight, contract_rows, preferred_element_type=jnp.float32
    )
    _, gelu_pull = jax.vjp(partial(jax.nn.gelu, approximate=False), pre_act)
    pre_grad = gelu_pull(act_grad)[0].astype(jnp.bfloat16)
    down_term = lax.dot_general(
        hidden, embed_grad, contract_first, preferred_element_type=jnp.float32
    )
    down_grad = lax.psum_scatter(down_term, "wide", scatter_dimension=1, tiled=True)
    up_grad = lax.psum_scatter(
        lax.dot_general(
            documents, pre_grad, contract_first, preferred_element_type=jnp.float32
        ).astype(jnp.bfloat16),
        "wide",
        scatter_dimension=0,
        tiled=True,
    ).astype(jnp.float32)
    return (label_grad, up_grad, down_grad)


def solution(mesh):
    in_specs = (
        P("wide", None),
        P(("wide", "narrow"), None),
        P(("wide", "narrow")),
        P("wide", None),
        P(None, "narrow"),
        P("narrow", None),
    )
    out_specs = (P(("wide", "narrow"), None), P("wide", "narrow"), P("narrow", "wide"))
    return jax.shard_map(local, mesh=mesh, in_specs=in_specs, out_specs=out_specs, check_vma=False)
```

profile of v0, /device:TPU:0, one launch (start us, length us, event | category | flops | bytes accessed | tf_op | source)
XLA Modules:
  0.0 531.9 jit_solution(12688162142580217697)
XLA Ops:
  7.2 1.2 copy-done
  8.4 10.4 %multiply_convert_fusion = (bf16[1024,768]{1,0:T(8,128)(2,1)S(1)}, f32[1024,768]{1,0:T(8,128)}, f32[1024,768]{1,0:T(8,128)}) fusion(bf16[1024,768]{1,0:T(8,128)(2,1)} %param.10, bf16[768,768]{1,0:T(8,128)(2,1)S(1)} %copy-done), kind=kOutput, calls=%fused_computation.38 | convolution fusion | flops 1259077632 | bytes 10616832 | tf_op jit(solution)/shard_map/dot_general | solution.py:45
  18.8 1.1 copy-done.8
  20.0 3.1 fusion.59
  23.7 10.2 %all-gather = s32[8,1,128]{2,1,0:T(1,128)S(1)} all-gather(s32[1,1,128]{2,1,0:T(1,128)S(1)} %bitcast.93), channel_id=1, replica_groups=mesh['wide'=8,'narrow'=4] {'wide'}, dimensions={0}, use_global_device_ids=true | all-gather | bytes 4608 | tf_op jit(solution)/shard_map/all_gather | solution.py:50
  34.1 1.7 convert_reduce_fusion.1
  35.8 111.2 %all-reduce.3.cloned.1.call-done = f32[1024,768]{1,0:T(8,128)} async-done(((f32[1024,768]{1,0:T(8,128)}), f32[1024,768]{1,0:T(8,128)}) %all-reduce.3.cloned.1.call-update) | async-done | bytes 3145744 | tf_op jit(solution)/shard_map/psum | solution.py:48
  147.0 2.7 add_convert_fusion.1
  149.7 1.3 broadcast_in_dim.59
  151.0 39.1 %while.42 = (s32[]{:T(128)}, bf16[64,768]{1,0:T(8,128)(2,1)S(1)}, bf16[64,768]{1,0:T(8,128)(2,1)S(1)}, bf16[8,128,768]{2,1,0:T(8,128)(2,1)}, f32[1024]{0:T(1024)...) while((s32[]{:T(128)}, bf16[64,768]{1,0:T(8,128)(2,1)S(1)}, ...), condition=%wide.region_4.5_spmd.clone, body=%wide.region_1.4_spmd.clone.sunk | while | flops 202249376 | bytes 4449310 | solution.py:90
  151.1 2.7 collective-permute-start.1
  157.0 1.9 collective-permute-start.1
  162.2 1.8 collective-permute-start.1
  166.6 1.0 collective-permute-start
  167.6 1.7 collective-permute-start.1
  172.3 1.1 collective-permute-start
  173.4 1.7 collective-permute-start.1
  179.1 2.0 collective-permute-start.1
  184.2 1.1 collective-permute-start
  185.3 1.6 collective-permute-start.1
  190.2 1.4 fusion.58
  191.6 9.2 %pmax.7 = f32[1024]{0:T(1024)S(1)} all-reduce(f32[1024]{0:T(1024)S(1)} %max.15), channel_id=1, replica_groups=mesh['wide'=8,'narrow'=4] {'narrow'}, use_global_device_ids=true, to_apply=%region_6.7 | all-reduce | flops 1024 | bytes 8192 | tf_op jit(solution)/shard_map/pmax | solution.py:104
  200.8 1.1 exponential_reduce_fusion.1
  202.0 9.5 %psum.22 = f32[1024]{0:T(1024)S(1)} all-reduce(f32[1024]{0:T(1024)S(1)} %exponential_multiply_fusion), channel_id=1, replica_groups=mesh['wide'=8,'narrow'=4] {'narrow'}, use_global_device_ids=true, to_apply=%region_8.9 | all-reduce | flops 1024 | bytes 8192 | tf_op jit(solution)/shard_map/psum | solution.py:105
  212.8 2.4 fusion.30
  216.0 104.4 %while.43 = (s32[]{:T(128)}, f32[128,768]{1,0:T(8,128)}, f32[1024,768]{1,0:T(8,128)}, s32[]{:T(128)}, bf16[8,128,768]{2,1,0:T(8,128)(2,1)}, /*index=5*/bf16[1024...) while((s32[]{:T(128)}, f32[128,768]{1,0:T(8,128)}, ...), condition=%wide.region_11.12_spmd.clone, body=%wide.region_9.11_spmd.clone.sunk | while | flops 607748224 | bytes 16669638 | solution.py:136
  216.9 1.0 copy.23
  217.9 1.8 fusion.99
  219.7 2.1 convolution_add_fusion.4
  221.9 3.2 select_add_fusion.2
  225.1 5.1 collective-permute-done.2
  232.8 1.8 fusion.99
  234.6 2.1 convolution_add_fusion.4
  236.8 4.3 select_add_fusion.2
  241.1 4.0 collective-permute-done.2
  247.7 1.8 fusion.99
  249.6 2.1 convolution_add_fusion.4
  251.7 4.3 select_add_fusion.2
  256.0 4.0 collective-permute-done.2
  262.6 1.8 fusion.99
  264.5 2.1 convolution_add_fusion.4
  266.6 4.3 select_add_fusion.2
  270.9 4.0 collective-permute-done.2
  277.5 1.8 fusion.99
  279.4 2.1 convolution_add_fusion.4
  281.5 4.3 select_add_fusion.2
  285.8 4.0 collective-permute-done.2
  292.5 1.8 fusion.99
  294.3 2.1 convolution_add_fusion.4
  296.4 4.3 select_add_fusion.2
  300.7 4.0 collective-permute-done.2
  307.4 1.8 fusion.99
  309.2 2.1 convolution_add_fusion.4
  311.3 4.3 select_add_fusion.2
  315.6 4.0 collective-permute-done.2
  320.4 4.3 convolution_add_fusion.1
  324.7 104.0 %all-reduce.4 = bf16[1024,768]{1,0:T(8,128)(2,1)} all-reduce(f32[1024,768]{1,0:T(8,128)} %convolution_add_fusion.1), channel_id=1, replica_groups=mesh['wide'=8,'narrow'=4] {'narrow'}, use_global_device_ids=true, to_apply=%region_13.14 | all-reduce | flops 786432 | bytes 4718592 | tf_op jit(solution)/shard_map/psum | solution.py:144
  428.7 10.2 %fusion.26 = bf16[768,768]{0,1:T(8,128)(2,1)} fusion(bf16[1024,768]{1,0:T(8,128)(2,1)} %param.10, f32[1024,768]{1,0:T(8,128)} %get-tuple-element.618, f32[1024,768]{1,0:T(8,128)} %get-tuple-element.630, bf16[768,768]{1,0:T(8,128)(2,1)} %param.15, bf16[1024,768]{1,0:T(8,128)(2,1)} %all-reduce.4), kind=kOutput, calls=%fused_computation.56 | convolution fusion | flops 2427518976 | bytes 11796480 | tf_op jit(solution)/shard_map/dot_general | solution.py:155
  438.9 2.4 copy.20
  441.4 4.8 fusion.60
  446.2 1.2 convolution_add_fusion.2
  447.3 31.2 %reduce-scatter.7.cloned.1.call-done = bf16[96,768]{1,0:T(8,128)(2,1)} async-done(((bf16[768,768]{1,0:T(8,128)(2,1)}), bf16[96,768]{1,0:T(8,128)(2,1)}) %reduce-scatter.7.cloned.1.call-update) | async-done | bytes 147472
  478.5 1.1 copy.21
  480.5 44.9 %reduce-scatter.5.cloned.1.call-done = f32[768,96]{0,1:T(8,128)} async-done(((f32[768,768]{0,1:T(8,128)}), f32[768,96]{0,1:T(8,128)}) %reduce-scatter.5.cloned.1.call-update) | async-done | bytes 294928 | tf_op jit(solution)/shard_map/reduce_scatter | solution.py:153
  (186 shorter events, 43.5 us)
Async XLA Ops:
  7.2 1.3 copy-start
  7.2 12.8 %copy-start.7 = (bf16[768,768]{1,0:T(8,128)(2,1)S(1)}, bf16[768,768]{1,0:T(8,128)(2,1)}, u32[]{:S(2)}) copy-start(bf16[768,768]{1,0:T(8,128)(2,1)} %param.15) | copy-start | bytes 3538948
  7.2 139.8 %all-reduce.3.cloned.1.call-start = ((), (), s32[]{:S(2)}) async-start(), calls=%async_computation.2 | async-start | bytes 6291456 | tf_op jit(solution)/shard_map/psum | solution.py:48
  18.8 1.1 copy-start.8
  23.1 0.7 copy-start.6
  23.1 11.0 %copy-start.4 = (s32[1024,4]{0,1:T(4,128)S(1)}, s32[1024,4]{0,1:T(4,128)}, u32[]{:S(2)}) copy-start(s32[1024,4]{0,1:T(4,128)} %param.13) | copy-start | bytes 49156
  23.1 12.7 %copy-start.5 = (bf16[128,768]{1,0:T(8,128)(2,1)S(1)}, bf16[128,768]{1,0:T(8,128)(2,1)}, u32[]{:S(2)}) copy-start(bf16[128,768]{1,0:T(8,128)(2,1)} %param.11) | copy-start | bytes 589828
  23.1 455.4 %reduce-scatter.7.cloned.1.call-start = ((), (), s32[]{:S(2)}) async-start(), calls=%async_computation.4 | async-start | bytes 1327104
  151.0 5.0 collective-permute-start
  151.1 4.9 collective-permute-start.1
  156.1 5.1 collective-permute-start
  157.0 4.2 collective-permute-start.1
  161.2 5.4 %collective-permute-start = (bf16[64,768]{1,0:T(8,128)(2,1)S(1)}, bf16[64,768]{1,0:T(8,128)(2,1)S(1)}, u32[]{:S(2)}, u32[]{:S(2)}) collective-permute-start(bf16[64,768]{1,0:T(8,128)(2,1)S(1)} %copy.34), channel_id=1, source_target_pairs={{28,0},{0,4},{4,8},{8,12},{12,16},{16,20},{20,24},{24,28},{29,1},{... | collective-permute-start | bytes 294920 | tf_op jit(solution)/shard_map/while/body/eval_jaxpr/ppermute | solution.py:14
  162.2 4.4 collective-permute-start.1
  166.6 5.7 %collective-permute-start = (bf16[64,768]{1,0:T(8,128)(2,1)S(1)}, bf16[64,768]{1,0:T(8,128)(2,1)S(1)}, u32[]{:S(2)}, u32[]{:S(2)}) collective-permute-start(bf16[64,768]{1,0:T(8,128)(2,1)S(1)} %copy.34), channel_id=1, source_target_pairs={{28,0},{0,4},{4,8},{8,12},{12,16},{16,20},{20,24},{24,28},{29,1},{... | collective-permute-start | bytes 294920 | tf_op jit(solution)/shard_map/while/body/eval_jaxpr/ppermute | solution.py:14
  167.6 4.7 collective-permute-start.1
  172.3 5.9 %collective-permute-start = (bf16[64,768]{1,0:T(8,128)(2,1)S(1)}, bf16[64,768]{1,0:T(8,128)(2,1)S(1)}, u32[]{:S(2)}, u32[]{:S(2)}) collective-permute-start(bf16[64,768]{1,0:T(8,128)(2,1)S(1)} %copy.34), channel_id=1, source_target_pairs={{28,0},{0,4},{4,8},{8,12},{12,16},{16,20},{20,24},{24,28},{29,1},{... | collective-permute-start | bytes 294920 | tf_op jit(solution)/shard_map/while/body/eval_jaxpr/ppermute | solution.py:14
  173.4 4.9 collective-permute-start.1
  178.3 5.9 %collective-permute-start = (bf16[64,768]{1,0:T(8,128)(2,1)S(1)}, bf16[64,768]{1,0:T(8,128)(2,1)S(1)}, u32[]{:S(2)}, u32[]{:S(2)}) collective-permute-start(bf16[64,768]{1,0:T(8,128)(2,1)S(1)} %copy.34), channel_id=1, source_target_pairs={{28,0},{0,4},{4,8},{8,12},{12,16},{16,20},{20,24},{24,28},{29,1},{... | collective-permute-start | bytes 294920 | tf_op jit(solution)/shard_map/while/body/eval_jaxpr/ppermute | solution.py:14
  179.1 5.1 collective-permute-start.1
  184.2 5.9 %collective-permute-start = (bf16[64,768]{1,0:T(8,128)(2,1)S(1)}, bf16[64,768]{1,0:T(8,128)(2,1)S(1)}, u32[]{:S(2)}, u32[]{:S(2)}) collective-permute-start(bf16[64,768]{1,0:T(8,128)(2,1)S(1)} %copy.34), channel_id=1, source_target_pairs={{28,0},{0,4},{4,8},{8,12},{12,16},{16,20},{20,24},{24,28},{29,1},{... | collective-permute-start | bytes 294920 | tf_op jit(solution)/shard_map/while/body/eval_jaxpr/ppermute | solution.py:14
  185.3 4.8 collective-permute-start.1
  221.9 8.3 %collective-permute-start.2 = (f32[128,768]{1,0:T(8,128)}, f32[128,768]{1,0:T(8,128)S(1)}, u32[]{:S(2)}, u32[]{:S(2)}) collective-permute-start(f32[128,768]{1,0:T(8,128)} %convolution_add_fusion.4), channel_id=1, source_target_pairs={{28,0},{0,4},{4,8},{8,12},{12,16},{16,20},{20,24},{24,28},{29,1},{... | collective-permute-start | bytes 1179656 | tf_op jit(solution)/shard_map/while/body/eval_jaxpr/ppermute | solution.py:14
  230.2 0.7 copy-start.1
  236.8 8.3 %collective-permute-start.2 = (f32[128,768]{1,0:T(8,128)}, f32[128,768]{1,0:T(8,128)S(1)}, u32[]{:S(2)}, u32[]{:S(2)}) collective-permute-start(f32[128,768]{1,0:T(8,128)} %convolution_add_fusion.4), channel_id=1, source_target_pairs={{28,0},{0,4},{4,8},{8,12},{12,16},{16,20},{20,24},{24,28},{29,1},{... | collective-permute-start | bytes 1179656 | tf_op jit(solution)/shard_map/while/body/eval_jaxpr/ppermute | solution.py:14
  245.1 0.7 copy-start.1
  251.7 8.3 %collective-permute-start.2 = (f32[128,768]{1,0:T(8,128)}, f32[128,768]{1,0:T(8,128)S(1)}, u32[]{:S(2)}, u32[]{:S(2)}) collective-permute-start(f32[128,768]{1,0:T(8,128)} %convolution_add_fusion.4), channel_id=1, source_target_pairs={{28,0},{0,4},{4,8},{8,12},{12,16},{16,20},{20,24},{24,28},{29,1},{... | collective-permute-start | bytes 1179656 | tf_op jit(solution)/shard_map/while/body/eval_jaxpr/ppermute | solution.py:14
  260.0 0.7 copy-start.1
  266.6 8.3 %collective-permute-start.2 = (f32[128,768]{1,0:T(8,128)}, f32[128,768]{1,0:T(8,128)S(1)}, u32[]{:S(2)}, u32[]{:S(2)}) collective-permute-start(f32[128,768]{1,0:T(8,128)} %convolution_add_fusion.4), channel_id=1, source_target_pairs={{28,0},{0,4},{4,8},{8,12},{12,16},{16,20},{20,24},{24,28},{29,1},{... | collective-permute-start | bytes 1179656 | tf_op jit(solution)/shard_map/while/body/eval_jaxpr/ppermute | solution.py:14
  274.9 0.7 copy-start.1
  281.5 8.3 %collective-permute-start.2 = (f32[128,768]{1,0:T(8,128)}, f32[128,768]{1,0:T(8,128)S(1)}, u32[]{:S(2)}, u32[]{:S(2)}) collective-permute-start(f32[128,768]{1,0:T(8,128)} %convolution_add_fusion.4), channel_id=1, source_target_pairs={{28,0},{0,4},{4,8},{8,12},{12,16},{16,20},{20,24},{24,28},{29,1},{... | collective-permute-start | bytes 1179656 | tf_op jit(solution)/shard_map/while/body/eval_jaxpr/ppermute | solution.py:14
  289.8 0.7 copy-start.1
  296.4 8.3 %collective-permute-start.2 = (f32[128,768]{1,0:T(8,128)}, f32[128,768]{1,0:T(8,128)S(1)}, u32[]{:S(2)}, u32[]{:S(2)}) collective-permute-start(f32[128,768]{1,0:T(8,128)} %convolution_add_fusion.4), channel_id=1, source_target_pairs={{28,0},{0,4},{4,8},{8,12},{12,16},{16,20},{20,24},{24,28},{29,1},{... | collective-permute-start | bytes 1179656 | tf_op jit(solution)/shard_map/while/body/eval_jaxpr/ppermute | solution.py:14
  304.7 0.7 copy-start.1
  311.3 8.3 %collective-permute-start.2 = (f32[128,768]{1,0:T(8,128)}, f32[128,768]{1,0:T(8,128)S(1)}, u32[]{:S(2)}, u32[]{:S(2)}) collective-permute-start(f32[128,768]{1,0:T(8,128)} %convolution_add_fusion.4), channel_id=1, source_target_pairs={{28,0},{0,4},{4,8},{8,12},{12,16},{16,20},{20,24},{24,28},{29,1},{... | collective-permute-start | bytes 1179656 | tf_op jit(solution)/shard_map/while/body/eval_jaxpr/ppermute | solution.py:14
  319.6 0.7 copy-start.1
  441.3 4.9 copy-start.2
  441.3 4.9 copy-start.3
  441.3 84.0 %reduce-scatter.5.cloned.1.call-start = ((), (), s32[]{:S(2)}) async-start(), calls=%async_computation.3 | async-start | bytes 2654208 | tf_op jit(solution)/shard_map/reduce_scatter | solution.py:153
Sparse Core Ops, SparseCore 0:
  23.2 123.7 all-reduce.2
  441.4 37.0 reduce-scatter.6
  482.8 42.4 reduce-scatter.4
where the time goes:
time: 533 us; the launch traced here: 532 us
  waiting for transfers between devices  220 us (41%)
  blocking collectives  133 us (25%)
  matrix products  99 us (19%)
  local copies, waits for them, and re-layouts  32.5 us (6%)
  starting transfers between devices  19.4 us (4%)
  between operations  13.9 us (3%)
  other arithmetic  13.2 us (2%)
    psum x1, waiting for transfers between devices, local(): summed = lax.psum(partial_out, 'narrow')  111 us
    psum x1, blocking collectives, local(): embed_grad = lax.psum(embed_back, 'narrow').astype(jnp.bfloat16)  104 us
    reduce_scatter x1, waiting for transfers between devices, local(): lax.psum_scatter(down_term, 'wide', scatter_dimension=1, tiled=True)  44.9 us
    ppermute x21, waiting for transfers between devices, from_behind(): return lax.ppermute(block, axis, route)  33.1 us
    unnamed x4, waiting for transfers between devices  31.2 us
    dot_general x7, matrix products, carry_home(): jnp.dot(grad_logits, label_block, preferred_element_type=jnp.float32)  29.1 us
    dot_general x16, matrix products, block_logits(): lax.dot_general(embedding, label_block, contract_rows, preferred_element_...  21.2 us
    ppermute x21, starting transfers between devices, from_behind(): return lax.ppermute(block, axis, route)  19.3 us
  transfers between devices with their start and end apart: 24, of which 16 were waited for; matrix products, arithmetic and copies ran while one was open for 10% of the time, Pallas kernels for 0%

commit v1 on v0

v1 whole, which is shorter than its diff:
```python
import functools

import jax
import jax.numpy as jnp
from jax import lax
from jax.experimental import pallas as pl
from jax.experimental.pallas import tpu as pltpu
from jax.sharding import PartitionSpec as P

CATALOG = 2812281
MESH = pl.DeviceIdType.MESH
F32 = jnp.float32
BF16 = jnp.bfloat16
CHUNK = 256
PIECE = 64
LAG = 2
NN = (((1,), (0,)), ((), ()))
NT = (((1,), (1,)), ((), ()))
TN = (((0,), (0,)), ((), ()))


def dot(a, b, dims):
    return lax.dot_general(a, b, dims, preferred_element_type=F32)


def kernel(
    nw, nn, per_doc,
    docs, label, log_exp, pos, up, down,
    label_out, up_out, down_out,
    labels, log_all, log_col, hidden, slope, own, emb, expo, grad, stat, stat_all,
    up_in, up_send, dn_in, dn_send, up_in2, up_send2, dn_in2, dn_send2,
    own2, embed_grad, label_acc, label_send, label_recv, up_acc, down_acc, pair_send, pair_recv,
    final_send, final_recv,
    g_send, g_recv, l_send, l_recv, s_send, s_recv,
    us_sem, ur_sem, ds_sem, dr_sem, us2_sem, ur2_sem, ds2_sem, dr2_sem,
    hs_sem, hr_sem, ps_sem, pr_sem, fs_sem, fr_sem,
):
    rows = docs.shape[0]
    lab = label.shape[0]
    chunks, pieces = rows // CHUNK, rows // PIECE
    per_chunk = CHUNK // PIECE
    wide = lax.axis_index("wide")
    me = lax.axis_index("narrow")

    barrier = pltpu.get_barrier_semaphore()

    @pl.loop(1, nw)
    def _(r):
        pl.semaphore_signal(barrier, inc=1, device_id={"wide": lax.rem(wide + r, nw)}, device_id_type=MESH)

    @pl.loop(1, nn)
    def _(r):
        pl.semaphore_signal(barrier, inc=1, device_id={"narrow": lax.rem(me + r, nn)}, device_id_type=MESH)

    pl.semaphore_wait(barrier, nw + nn - 2)

    def remote(src, dst, send, recv, **device):
        return pltpu.make_async_remote_copy(
            src_ref=src, dst_ref=dst, send_sem=send, recv_sem=recv, device_id=device, device_id_type=MESH
        )

    def label_copy(r):
        return remote(label, labels.at[pl.ds(pl.multiple_of(wide * lab, lab), lab)], g_send.at[r], g_recv.at[wide],
                      wide=lax.rem(wide + r, nw))

    def log_copy(r):
        return remote(log_exp, log_all.at[wide], l_send.at[r], l_recv.at[wide], wide=lax.rem(wide + r, nw))

    @pl.loop(1, nw)
    def _(r):
        log_copy(r).start()
        label_copy(r).start()

    labels[pl.ds(pl.multiple_of(wide * lab, lab), lab), :] = label[...]
    log_all[wide] = log_exp[...]

    def chunk_of(c):
        return pl.ds(pl.multiple_of(c * CHUNK, CHUNK), CHUNK)

    def piece_of(p):
        return pl.ds(pl.multiple_of(p * PIECE, PIECE), PIECE)

    def forward(c):
        at = chunk_of(c)
        pre = dot(docs[at, :], up[...], NN)
        cdf = 0.5 * (1.0 + lax.erf(pre * 0.7071067811865476))
        slope[at, :] = cdf + pre * jnp.exp(-0.5 * pre * pre) * 0.3989422804014327
        mid = (pre * cdf).astype(BF16)
        hidden[at, :] = mid
        own[at, :] = dot(mid, down[...], NN)

    def scan_step(t, terms, u_in, u_send, d_in, d_send, us, ur, ds, dr, finish):
        def one(p, first, last, inbox, outbox, send, recv, target):
            at = piece_of(p)

            @pl.when((p >= 0) & (p < pieces))
            def _():
                @pl.when(jnp.logical_not(first))
                def _():
                    remote(outbox.at[at], inbox.at[at], send.at[p], recv.at[p], narrow=target).wait_recv()

                @pl.when(jnp.logical_not(last))
                def _():
                    @pl.when(first)
                    def _():
                        outbox[at, :] = terms[at, :].astype(BF16)

                    @pl.when(jnp.logical_not(first))
                    def _():
                        outbox[at, :] = (terms[at, :] + inbox[at, :].astype(F32)).astype(BF16)

                    remote(outbox.at[at], inbox.at[at], send.at[p], recv.at[p], narrow=target).start()

        low, high = me == 0, me == nn - 1
        one(t - LAG * me, low, high, u_in, u_send, us, ur, lax.rem(me + 1, nn))
        one(t - LAG * (nn - 1 - me), high, low, d_in, d_send, ds, dr, lax.rem(me + nn - 1, nn))
        q = t - LAG * jnp.maximum(me, nn - 1 - me)
        at = piece_of(q)

        @pl.when((q >= 0) & (q < pieces))
        def _():
            @pl.when(low)
            def _():
                finish(at, terms[at, :] + d_in[at, :].astype(F32))

            @pl.when(high)
            def _():
                finish(at, terms[at, :] + u_in[at, :].astype(F32))

            @pl.when(jnp.logical_not(low | high))
            def _():
                finish(at, terms[at, :] + u_in[at, :].astype(F32) + d_in[at, :].astype(F32))

        return q

    def drain(outbox, inbox, send, recv, skip):
        @pl.when(jnp.logical_not(skip))
        def _():
            @pl.loop(0, pieces)
            def _(p):
                at = piece_of(p)
                remote(outbox.at[at], inbox.at[at], send.at[p], recv.at[p], narrow=lax.rem(me + 1, nn)).wait_send()

    def when_chunk(q, act):
        done = (q >= 0) & (q < pieces) & (lax.rem(q + pieces, per_chunk) == per_chunk - 1)

        @pl.when(done)
        def _():
            act(q // per_chunk)

    def tile(w):
        return pl.ds(pl.multiple_of(w * lab, lab), lab)

    def stat_copy(r, c):
        return remote(stat.at[c], stat_all.at[me, c], s_send.at[r, c], s_recv.at[me, c], narrow=lax.rem(me + r, nn))

    def logits(c):
        @pl.when(c == 0)
        def _():
            @pl.loop(1, nw)
            def _(r):
                src = lax.rem(wide + r, nw)
                remote(label, labels.at[tile(src)], g_send.at[r], g_recv.at[src], wide=src).wait_recv()
                remote(log_exp, log_all.at[src], l_send.at[r], l_recv.at[src], wide=src).wait_recv()

            @pl.loop(0, nw)
            def _(w):
                log_col[tile(w), :] = jnp.broadcast_to(log_all[w][0:1, :], (lab, lab)).T

        expo[c] = dot(labels[...], emb[chunk_of(c), :], NT)

        def top(w, best):
            part = expo[c, tile(w), :] - log_col[tile(w), 0:1]
            expo[c, tile(w), :] = part
            return jnp.maximum(best, jnp.max(part, axis=0, keepdims=True))

        best = lax.fori_loop(0, nw, top, jnp.full((1, CHUNK), -jnp.inf, F32))

        def add(w, total):
            part = jnp.exp(expo[c, tile(w), :] - best)
            expo[c, tile(w), :] = part
            return total + jnp.sum(part, axis=0, keepdims=True)

        total = lax.fori_loop(0, nw, add, jnp.zeros((1, CHUNK), F32))
        stat[c, 0:1, :] = best
        stat[c, 1:2, :] = total

        @pl.loop(1, nn)
        def _(r):
            stat_copy(r, c).start()

    def finish_embedding(at, value):
        emb[at, :] = (docs[at, :].astype(F32) + value).astype(BF16)

    steps = pieces + LAG * (nn - 1)
    stat[...] = jnp.zeros_like(stat)
    forward(0)

    @pl.loop(0, steps)
    def _(t):
        q = scan_step(t, own, up_in, up_send, dn_in, dn_send, us_sem, ur_sem, ds_sem, dr_sem, finish_embedding)

        @pl.when(t < chunks - 1)
        def _():
            forward(t + 1)

        when_chunk(q, logits)

    def gradient(c):
        @pl.loop(1, nn)
        def _(r):
            src = lax.rem(me + r, nn)
            remote(stat.at[c], stat_all.at[src, c], s_send.at[r, c], s_recv.at[src, c], narrow=src).wait_recv()

        mine, mine_sum = stat[c, 0:1, :], stat[c, 1:2, :]
        top = lax.fori_loop(
            1, nn, lambda r, m: jnp.maximum(m, stat_all[lax.rem(me + r, nn), c, 0:1, :]), mine
        )

        def add(r, s):
            src = lax.rem(me + r, nn)
            return s + stat_all[src, c, 1:2, :] * jnp.exp(stat_all[src, c, 0:1, :] - top)

        shrink = jnp.exp(mine - top)
        scale = shrink / lax.fori_loop(1, nn, add, mine_sum * shrink)
        offsets = lax.broadcasted_iota(jnp.int32, (lab, CHUNK), 0)

        @pl.loop(0, nw)
        def _(w):
            columns = offsets + (w * nn + me) * lab
            hits = jnp.zeros((lab, CHUNK), F32)
            for k in range(per_doc):
                hits = hits + jnp.where(pos[c, k : k + 1, :] == columns, 1.0, 0.0)
            grad[tile(w), :] = (expo[c, tile(w), :] * scale - hits / per_doc).astype(BF16)

        own2[chunk_of(c), :] = dot(grad[...], labels[...], TN)

    def label_part(c):
        label_acc[...] += dot(grad[...], emb[chunk_of(c), :], NN)

    def home_copy(r):
        to = lax.rem(wide + r, nw)
        return remote(label_send.at[tile(to)], label_recv.at[tile(wide)], hs_sem.at[r], hr_sem.at[wide], wide=to)

    def finish_gradient(at, value):
        embed_grad[at, :] = value.astype(BF16)

    def backward(c):
        at = chunk_of(c)
        back = embed_grad[at, :]
        pre_grad = (dot(back, down[...], NT) * slope[at, :]).astype(BF16)
        up_acc[...] += dot(docs[at, :], pre_grad, TN)
        down_acc[...] += dot(back, hidden[at, :], TN)

    label_acc[...] = jnp.zeros_like(label_acc)
    up_acc[...] = jnp.zeros_like(up_acc)
    down_acc[...] = jnp.zeros_like(down_acc)
    gradient(0)

    @pl.loop(0, steps)
    def _(t):
        q = scan_step(
            t, own2, up_in2, up_send2, dn_in2, dn_send2, us2_sem, ur2_sem, ds2_sem, dr2_sem, finish_gradient
        )

        @pl.when(t < chunks)
        def _():
            label_part(t)

        @pl.when(t < chunks - 1)
        def _():
            gradient(t + 1)

        @pl.when(t == chunks - 1)
        def _():
            label_send[...] = label_acc[...].astype(BF16)

            @pl.loop(1, nw)
            def _(r):
                home_copy(r).start()

        when_chunk(q, backward)

    blk = up_acc.shape[0] // nw
    half = nw // 2
    side = lax.rem(wide, 2)
    other = wide + 1 - 2 * side

    def block(b):
        return pl.ds(pl.multiple_of(b * blk, blk), blk)

    def pair_copy(i):
        return remote(pair_send.at[i], pair_recv.at[i], ps_sem.at[i], pr_sem.at[i], wide=other)

    def final_copy(r):
        i = lax.rem(wide // 2 + r, half)
        return remote(final_send.at[i], final_recv.at[wide // 2], fs_sem.at[r], fr_sem.at[wide // 2],
                      wide=2 * i + side)

    @pl.loop(0, half)
    def _(r):
        i = lax.rem(wide // 2 + 1 + r, half)
        b = 2 * i + 1 - side
        pair_send[i, 0:blk, :] = up_acc[block(b), :].astype(BF16)
        pair_send[i, blk:, :] = down_acc[block(b), :].astype(BF16)
        pair_copy(i).start()

    @pl.loop(1, half)
    def _(r):
        i = lax.rem(wide // 2 + r, half)
        b = 2 * i + side
        pair_copy(i).wait_recv()
        final_send[i, 0:blk, :] = (up_acc[block(b), :] + pair_recv[i, 0:blk, :].astype(F32)).astype(BF16)
        final_send[i, blk:, :] = (down_acc[block(b), :] + pair_recv[i, blk:, :].astype(F32)).astype(BF16)
        final_copy(r).start()

    label_out[...] = label_acc[tile(wide), :]

    @pl.loop(1, nw)
    def _(r):
        src = lax.rem(wide + r, nw)
        remote(label_send.at[tile(src)], label_recv.at[tile(src)], hs_sem.at[r], hr_sem.at[src], wide=src).wait_recv()
        label_out[...] += label_recv[tile(src), :].astype(F32)

    mine = wide // 2
    pair_copy(mine).wait_recv()
    up_out[...] = up_acc[block(wide), :] + pair_recv[mine, 0:blk, :].astype(F32)
    down_out[...] = down_acc[block(wide), :] + pair_recv[mine, blk:, :].astype(F32)

    @pl.loop(1, half)
    def _(r):
        i = lax.rem(mine + r, half)
        remote(final_send.at[i], final_recv.at[i], fs_sem.at[r], fr_sem.at[i], wide=2 * i + side).wait_recv()
        up_out[...] += final_recv[i, 0:blk, :].astype(F32)
        down_out[...] += final_recv[i, blk:, :].astype(F32)

    low, high = me == 0, me == nn - 1
    drain(up_send, up_in, us_sem, ur_sem, high)
    drain(dn_send, dn_in, ds_sem, dr_sem, low)
    drain(up_send2, up_in2, us2_sem, ur2_sem, high)
    drain(dn_send2, dn_in2, ds2_sem, dr2_sem, low)

    @pl.loop(1, nw)
    def _(r):
        label_copy(r).wait_send()
        log_copy(r).wait_send()
        home_copy(r).wait_send()

    @pl.loop(1, nn)
    def _(r):
        @pl.loop(0, chunks)
        def _(c):
            stat_copy(r, c).wait_send()

    @pl.loop(0, half)
    def _(i):
        pair_copy(i).wait_send()

    @pl.loop(1, half)
    def _(r):
        final_copy(r).wait_send()


def expected_log(rank_ids, sampled):
    rank_float = rank_ids.astype(F32)
    return (
        jnp.log(F32(sampled))
        + jnp.log(jnp.log1p(1.0 / (rank_float + 1.0)))
        - jnp.log(jnp.log(F32(CATALOG) + 1.0))
    )


def local(documents, label_weight, sample_ids, positive_cols, up_weight, down_weight):
    nw, nn = lax.axis_size("wide"), lax.axis_size("narrow")
    lab, width = label_weight.shape
    rows = documents.shape[0]
    ff = up_weight.shape[1]
    per_doc = positive_cols.shape[1]
    chunks, pieces = rows // CHUNK, rows // PIECE
    columns = lab * nw
    blk, half = width // nw, nw // 2
    log_exp = jnp.broadcast_to(expected_log(sample_ids, columns * nn)[None, :], (8, lab))
    pos = positive_cols.reshape(chunks, CHUNK, per_doc).transpose(0, 2, 1)
    V = pltpu.VMEM
    dma = pltpu.SemaphoreType.DMA
    wide_rows = [V((rows, width), BF16)] * 4
    label_grad, up_grad, down_grad = pl.pallas_call(
        functools.partial(kernel, nw, nn, per_doc),
        out_shape=[
            jax.ShapeDtypeStruct((lab, width), F32),
            jax.ShapeDtypeStruct((blk, ff), F32),
            jax.ShapeDtypeStruct((blk, ff), F32),
        ],
        in_specs=[pl.BlockSpec(memory_space=pltpu.VMEM)] * 6,
        out_specs=[pl.BlockSpec(memory_space=pltpu.VMEM)] * 3,
        scratch_shapes=[
            V((columns, width), BF16), V((nw, 8, lab), F32), V((columns, lab), F32),
            V((rows, ff), BF16), V((rows, ff), F32), V((rows, width), F32), V((rows, width), BF16),
            V((chunks, columns, CHUNK), F32), V((columns, CHUNK), BF16),
            V((chunks, 8, CHUNK), F32), V((nn, chunks, 8, CHUNK), F32),
            *wide_rows, *wide_rows,
            V((rows, width), F32), V((rows, width), BF16),
            V((columns, width), F32), V((columns, width), BF16), V((columns, width), BF16),
            V((width, ff), F32), V((width, ff), F32),
            V((half, 2 * blk, ff), BF16), V((half, 2 * blk, ff), BF16),
            V((half, 2 * blk, ff), BF16), V((half, 2 * blk, ff), BF16),
            dma((nw,)), dma((nw,)), dma((nw,)), dma((nw,)), dma((nn, chunks)), dma((nn, chunks)),
            *[dma((pieces,))] * 8,
            dma((nw,)), dma((nw,)), dma((half,)), dma((half,)), dma((half,)), dma((half,)),
        ],
        compiler_params=pltpu.CompilerParams(
            collective_id=0, has_side_effects=True, vmem_limit_bytes=60 * 1024 * 1024
        ),
    )(documents, label_weight, log_exp, pos, up_weight, down_weight)
    return (label_grad, up_grad, down_grad.T)


def solution(mesh):
    in_specs = (
        P("wide", None),
        P(("wide", "narrow"), None),
        P(("wide", "narrow")),
        P("wide", None),
        P(None, "narrow"),
        P("narrow", None),
    )
    out_specs = (P(("wide", "narrow"), None), P("wide", "narrow"), P("narrow", "wide"))
    return jax.shard_map(local, mesh=mesh, in_specs=in_specs, out_specs=out_specs, check_vma=False)
```

time: 533 us -> 131 us (0.25)
  waiting for transfers between devices: 220 us -> 0 us
  blocking collectives: 133 us -> 0 us
  Pallas kernels: 0 us -> 125 us
  matrix products: 99 us -> 0 us
  local copies, waits for them, and re-layouts: 32.5 us -> 4.83 us
  starting transfers between devices: 19.4 us -> 0 us
  between operations: 13.9 us -> 0.65 us
  other arithmetic: 13.2 us -> 0.67 us
    pallas_call x0 -> x1, Pallas kernels: none -> 125 us  [local(): pl.pallas_call(functools.partial(kernel, nw, nn, per_doc), out_shape=[jax...]
    psum x2 -> x0, blocking collectives: 114 us -> none  [the longest x1 104 us: local(): embed_grad = lax.psum(embed_back, 'narrow').astype(jnp.bfloat16)]
    psum x1 -> x0, waiting for transfers between devices: 111 us -> none  [local(): summed = lax.psum(partial_out, 'narrow')]
    dot_general x36 -> x0, matrix products: 99 us -> none  [the longest x7 29.1 us: carry_home(): jnp.dot(grad_logits, label_block, preferred_element_type=jnp.float32)]
    reduce_scatter x1 -> x0, waiting for transfers between devices: 44.9 us -> none  [local(): lax.psum_scatter(down_term, 'wide', scatter_dimension=1, tiled=True)]
    ppermute x21 -> x0, waiting for transfers between devices: 33.1 us -> none  [from_behind(): return lax.ppermute(block, axis, route)]
    unnamed x4 -> x0, waiting for transfers between devices: 31.2 us -> none
    ppermute x21 -> x0, starting transfers between devices: 19.3 us -> none  [from_behind(): return lax.ppermute(block, axis, route)]
  transfers between devices with their start and end apart: 24 -> 0, of which waited for: 16 -> 0; matrix products, arithmetic and copies ran while one was open for 10% -> 0% of each run, Pallas kernels for 0% -> 0%
where the time goes in v1:
time: 131 us
  Pallas kernels  125 us (95%)
  local copies, waits for them, and re-layouts  4.83 us (4%)
    pallas_call x1, Pallas kernels, local(): pl.pallas_call(functools.partial(kernel, nw, nn, per_doc), out_shape=[jax...  125 us
    unnamed x5, local copies, waits for them, and re-layouts  4.22 us

profile of v1, /device:TPU:0, one launch (start us, length us, event | category | flops | bytes accessed | tf_op | source)
XLA Modules:
  0.0 131.1 jit_solution(13106170083740758993)
XLA Ops:
  0.6 0.7 log_add_fusion
  1.3 0.6 broadcast_in_dim.2.log_exp
  1.9 124.9 %shard_map.85 = (f32[128,768]{1,0:T(8,128)}, f32[96,768]{1,0:T(8,128)}, f32[96,768]{1,0:T(8,128)}) custom-call(bf16[1024,768]{1,0:T(8,128)(2,1)} %docs.1, bf16[128,768]{1,0:T(8,128)(2,1)} %label.1, f32[8,128]{1,0:T(8,128)} %broadcast_in_dim.2.log_exp, s32[4,4,256]{2,1,0:T(4,128)} %bitcast.5, bf16[768,768]{1,0:T(8,128)(2,1)} %up.1, bf16[768,768]{1,0:T(8,128)(2,1)} %down.1), custom_call_target="tpu_custom_call" | custom-call | tf_op jit(solution)/shard_map/pallas_call | solution.py:387
  126.8 0.0 copy-start
  126.8 1.8 %copy.12 = f32[128,768]{1,0:T(8,128)} copy(f32[128,768]{1,0:T(8,128)} %get-tuple-element.12) | data formatting | bytes 786432
  128.7 1.7 %copy.13 = f32[96,768]{1,0:T(8,128)} copy(f32[96,768]{1,0:T(8,128)} %get-tuple-element.13) | data formatting | bytes 589824
  130.3 0.0 copy-done
  130.4 0.7 copy.14
Async XLA Ops:
  126.8 3.5 %copy-start = (f32[96,768]{1,0:T(8,128)S(1)}, f32[96,768]{1,0:T(8,128)}, u32[]{:S(2)}) copy-start(f32[96,768]{1,0:T(8,128)} %get-tuple-element.8) | copy-start | bytes 884740

commit v2 on v1

--- a/solution.py
+++ b/solution.py
@@ -13,7 +13,8 @@
 BF16 = jnp.bfloat16
 CHUNK = 256
 PIECE = 64
-LAG = 2
+LAG = 3
+STAT_LAG = 2
 NN = (((1,), (0,)), ((), ()))
 NT = (((1,), (1,)), ((), ()))
 TN = (((0,), (0,)), ((), ()))
@@ -192,19 +193,8 @@
     def finish_embedding(at, value):
         emb[at, :] = (docs[at, :].astype(F32) + value).astype(BF16)
 
-    steps = pieces + LAG * (nn - 1)
     stat[...] = jnp.zeros_like(stat)
     forward(0)
-
-    @pl.loop(0, steps)
-    def _(t):
-        q = scan_step(t, own, up_in, up_send, dn_in, dn_send, us_sem, ur_sem, ds_sem, dr_sem, finish_embedding)
-
-        @pl.when(t < chunks - 1)
-        def _():
-            forward(t + 1)
-
-        when_chunk(q, logits)
 
     def gradient(c):
         @pl.loop(1, nn)
@@ -255,23 +245,34 @@
     label_acc[...] = jnp.zeros_like(label_acc)
     up_acc[...] = jnp.zeros_like(up_acc)
     down_acc[...] = jnp.zeros_like(down_acc)
-    gradient(0)
-
-    @pl.loop(0, steps)
+    first_grad = per_chunk + LAG * (nn - 1) + STAT_LAG - 1
+    second = first_grad + 1
+
+    @pl.loop(0, second + pieces + LAG * (nn - 1))
     def _(t):
-        q = scan_step(
-            t, own2, up_in2, up_send2, dn_in2, dn_send2, us2_sem, ur2_sem, ds2_sem, dr2_sem, finish_gradient
+        q = scan_step(t, own, up_in, up_send, dn_in, dn_send, us_sem, ur_sem, ds_sem, dr_sem, finish_embedding)
+
+        @pl.when(t < chunks - 1)
+        def _():
+            forward(t + 1)
+
+        when_chunk(q, logits)
+        q2 = scan_step(
+            t - second, own2, up_in2, up_send2, dn_in2, dn_send2, us2_sem, ur2_sem, ds2_sem, dr2_sem,
+            finish_gradient,
         )
-
-        @pl.when(t < chunks)
-        def _():
-            label_part(t)
-
-        @pl.when(t < chunks - 1)
-        def _():
-            gradient(t + 1)
-
-        @pl.when(t == chunks - 1)
+        since = t - first_grad
+        turn = lax.rem(since + pieces, per_chunk)
+
+        @pl.when((since >= 0) & (since < pieces) & (turn == 0))
+        def _():
+            gradient(since // per_chunk)
+
+        @pl.when((since >= 0) & (since < pieces) & (turn == 1))
+        def _():
+            label_part(since // per_chunk)
+
+        @pl.when(since == pieces - per_chunk + 1)
         def _():
             label_send[...] = label_acc[...].astype(BF16)
 
@@ -279,7 +280,7 @@
             def _(r):
                 home_copy(r).start()
 
-        when_chunk(q, backward)
+        when_chunk(q2, backward)
 
     blk = up_acc.shape[0] // nw
     half = nw // 2

time: 131 us -> 118 us (0.901)
  Pallas kernels: 125 us -> 112 us
    pallas_call x1, Pallas kernels: 125 us -> 112 us  [local(): pl.pallas_call(functools.partial(kernel, nw, nn, per_doc), out_shape=[jax...]
where the time goes in v2:
time: 118 us
  Pallas kernels  112 us (95%)
  local copies, waits for them, and re-layouts  4.83 us (4%)
    pallas_call x1, Pallas kernels, local(): pl.pallas_call(functools.partial(kernel, nw, nn, per_doc), out_shape=[jax...  112 us
    unnamed x5, local copies, waits for them, and re-layouts  4.22 us

profile of v2, /device:TPU:0, one launch (start us, length us, event | category | flops | bytes accessed | tf_op | source)
XLA Modules:
  0.0 118.2 jit_solution(17065582100670773227)
XLA Ops:
  0.6 0.7 log_add_fusion
  1.3 0.6 broadcast_in_dim.2.log_exp
  1.9 112.1 %shard_map.85 = (f32[128,768]{1,0:T(8,128)}, f32[96,768]{1,0:T(8,128)}, f32[96,768]{1,0:T(8,128)}) custom-call(bf16[1024,768]{1,0:T(8,128)(2,1)} %docs.1, bf16[128,768]{1,0:T(8,128)(2,1)} %label.1, f32[8,128]{1,0:T(8,128)} %broadcast_in_dim.2.log_exp, s32[4,4,256]{2,1,0:T(4,128)} %bitcast.5, bf16[768,768]{1,0:T(8,128)(2,1)} %up.1, bf16[768,768]{1,0:T(8,128)(2,1)} %down.1), custom_call_target="tpu_custom_call" | custom-call | tf_op jit(solution)/shard_map/pallas_call | solution.py:388
  114.0 0.0 copy-start
  114.0 1.8 %copy.12 = f32[128,768]{1,0:T(8,128)} copy(f32[128,768]{1,0:T(8,128)} %get-tuple-element.12) | data formatting | bytes 786432
  115.8 1.7 %copy.13 = f32[96,768]{1,0:T(8,128)} copy(f32[96,768]{1,0:T(8,128)} %get-tuple-element.13) | data formatting | bytes 589824
  117.5 0.0 copy-done
  117.5 0.7 copy.14
Async XLA Ops:
  114.0 3.5 %copy-start = (f32[96,768]{1,0:T(8,128)S(1)}, f32[96,768]{1,0:T(8,128)}, u32[]{:S(2)}) copy-start(f32[96,768]{1,0:T(8,128)} %get-tuple-element.8) | copy-start | bytes 884740
